TPU v7x, 32 devices: a whole 2x2x4 slice. The times are simulated.
32 devices in a mesh: dp: 2 (over x), expert: 16 (over z, y, core).
Axes of the slice: x: 2, y: 2, z: 4, core: 2. Of those that a mesh axis runs over, the one named last changes fastest.
Arguments:
- tokens: bfloat16 [4096, 2048], P(('dp', 'expert')), may hold values from -6 to 6
- out_grad: bfloat16 [4096, 2048], P(('dp', 'expert')), may hold values from -6 to 6
- gate_saved: bfloat16 [4096, 6, 1408], P(('dp', 'expert')), may hold values from -6 to 6
- probs: float32 [4096, 6], P(('dp', 'expert')), may hold values from 0.1 to 1
- expert_ids: int32 [4096, 6], P(('dp', 'expert')), may hold values from 0 to 15, all different within a row; in each aligned block of 128 rows (0 to 127, 128 to 255, ...) at most 96 rows name the same one
- w_gate: bfloat16 [16, 2048, 1408], P('expert'), may hold values from -0.125 to 0.125
- w_up: bfloat16 [16, 2048, 1408], P('expert'), may hold values from -0.125 to 0.125
- w_down: bfloat16 [16, 1408, 2048], P('expert'), may hold values from -0.15625 to 0.15625
Outputs:
- input_grad: bfloat16 [4096, 2048], P(('dp', 'expert'))
- grad_gate: bfloat16 [16, 2048, 1408], P('expert', 'dp')
- grad_up: bfloat16 [16, 2048, 1408], P('expert', 'dp')
- grad_down: bfloat16 [16, 1408, 2048], P('expert', 'dp')
Inputs may be any that keep to these rules, and one draw needn't show every extreme that they name: `expert_ids`: each token names 6 different experts. Among the 128 tokens of one aligned block (the tokens of one device) no expert is named more than 96 times, and in some block some expert is named exactly 96 times.
All inputs are finite; a program needn't handle non-finite values.
Results may differ from a plain program's by a relative error of at most 0.013.
Values may be sent and summed in bfloat16 or wider, within the bound.
No kernel may reach another device: no remote copies, remote signals or barrier semaphores. Data moves between devices by JAX's collectives and lax.ppermute only.
A program may use at most 192 MiB of HBM per device.

v0:
```python
import jax
import jax.numpy as jnp
from jax import lax
from jax.sharding import PartitionSpec as P

grad_scale = 0.0625


def route_math(rows_in, routed_rows, gate_rows, gate_mat, up_mat, down_mat):
    contract_cols = (((1,), (1,)), ((), ()))
    up_act = jnp.dot(rows_in, up_mat, preferred_element_type=jnp.float32)
    gate_val = gate_rows.astype(jnp.float32)
    gate_sig = jax.nn.sigmoid(gate_val)
    gate_act = gate_val * gate_sig
    hidden_act = (gate_act * up_act).astype(jnp.bfloat16)
    hidden_grad = lax.dot_general(
        routed_rows, down_mat, contract_cols, preferred_element_type=jnp.float32
    )
    up_grad = (hidden_grad * gate_act).astype(jnp.bfloat16)
    gate_grad = (hidden_grad * up_act * gate_sig * (1.0 + gate_val * (1.0 - gate_sig))).astype(
        jnp.bfloat16
    )
    input_part = (
        lax.dot_general(gate_grad, gate_mat, contract_cols, preferred_element_type=jnp.float32)
        + lax.dot_general(up_grad, up_mat, contract_cols, preferred_element_type=jnp.float32)
    ).astype(jnp.bfloat16)
    return (input_part, gate_grad, up_grad, hidden_act)


def weight_terms(rows_in, routed_rows, gate_grad, up_grad, hidden_act):
    contract_rows = (((0,), (0,)), ((), ()))
    both_grads = jnp.concatenate([gate_grad, up_grad], axis=1)
    term_gate_up = lax.dot_general(
        rows_in, both_grads, contract_rows, preferred_element_type=jnp.float32
    )
    term_down = lax.dot_general(
        hidden_act, routed_rows, contract_rows, preferred_element_type=jnp.float32
    )
    return (term_gate_up, term_down)


def local(tokens, out_grad, gate_saved, probs, expert_ids, w_gate, w_up, w_down):
    n_peers = lax.axis_size("expert")
    tok_rows, model_width = tokens.shape
    top_k = expert_ids.shape[1]
    hidden_width = w_up.shape[2]
    slot_cap = min(tok_rows, 2 * tok_rows * top_k // n_peers)
    n_routes = tok_rows * top_k
    n_slots = n_peers * slot_cap
    row_block = 256
    padded_rows = -(-n_slots // row_block) * row_block
    flat_ids = expert_ids.reshape(n_routes)
    onehot = (flat_ids[:, None] == jnp.arange(n_peers, dtype=jnp.int32)[None, :]).astype(jnp.int32)
    slot_rank = jnp.sum((jnp.cumsum(onehot, axis=0) - 1) * onehot, axis=1)
    slot_of_route = flat_ids * slot_cap + slot_rank
    route_of_slot = (
        jnp.full((n_slots,), n_routes, jnp.int32)
        .at[slot_of_route]
        .set(jnp.arange(n_routes, dtype=jnp.int32))
    )
    used_slot = route_of_slot < n_routes
    safe_route = jnp.minimum(route_of_slot, n_routes - 1)
    token_of_slot = safe_route // top_k
    scaled = probs.reshape(n_routes)[safe_route][:, None] * out_grad[token_of_slot].astype(
        jnp.float32
    )
    send_grad = (
        jnp.where(used_slot[:, None], scaled, 0.0)
        .astype(jnp.bfloat16)
        .reshape(n_peers, slot_cap, model_width)
    )
    send_rows = jnp.where(used_slot[:, None], tokens[token_of_slot], 0).reshape(
        n_peers, slot_cap, model_width
    )
    send_gate = jnp.where(
        used_slot[:, None], gate_saved.reshape(n_routes, hidden_width)[safe_route], 0
    ).reshape(n_peers, slot_cap, hidden_width)
    gate_mat = w_gate[0]
    up_mat = w_up[0]
    down_mat = w_down[0]
    recv_rows, recv_grad, recv_gate = (
        lax.all_to_all(send_rows, "expert", split_axis=0, concat_axis=0, tiled=True),
        lax.all_to_all(send_grad, "expert", split_axis=0, concat_axis=0, tiled=True),
        lax.all_to_all(send_gate, "expert", split_axis=0, concat_axis=0, tiled=True),
    )
    recv_rows = recv_rows.reshape(n_slots, model_width)
    recv_grad = recv_grad.reshape(n_slots, model_width)
    recv_gate = recv_gate.reshape(n_slots, hidden_width)
    live_rows = jnp.any(recv_grad != 0, axis=1)
    dense_pos = jnp.where(live_rows, jnp.cumsum(live_rows.astype(jnp.int32)) - 1, padded_rows)
    n_live = jnp.sum(live_rows.astype(jnp.int32))
    dense_rows = (
        jnp.zeros((padded_rows, model_width), jnp.bfloat16)
        .at[dense_pos]
        .set(recv_rows, mode="drop")
    )
    dense_grad = (
        jnp.zeros((padded_rows, model_width), jnp.bfloat16)
        .at[dense_pos]
        .set(recv_grad, mode="drop")
    )
    dense_gate = (
        jnp.zeros((padded_rows, hidden_width), jnp.bfloat16)
        .at[dense_pos]
        .set(recv_gate, mode="drop")
    )
    n_blocks = (n_live + row_block - 1) // row_block

    def block_step(block_index, state):
        dense_out, acc_gate_up, acc_down = state
        first_row = block_index * row_block
        rows_in = lax.dynamic_slice_in_dim(dense_rows, first_row, row_block, 0)
        routed_rows = lax.dynamic_slice_in_dim(dense_grad, first_row, row_block, 0)
        gate_rows = lax.dynamic_slice_in_dim(dense_gate, first_row, row_block, 0)
        input_part, gate_grad, up_grad, hidden_act = route_math(
            rows_in, routed_rows, gate_rows, gate_mat, up_mat, down_mat
        )
        term_gate_up, term_down = weight_terms(rows_in, routed_rows, gate_grad, up_grad, hidden_act)
        dense_out = lax.dynamic_update_slice_in_dim(dense_out, input_part, first_row, 0)
        return (dense_out, acc_gate_up + term_gate_up, acc_down + term_down)

    start_state = (
        jnp.zeros((padded_rows, model_width), jnp.bfloat16),
        jnp.zeros((model_width, 2 * hidden_width), jnp.float32),
        jnp.zeros((hidden_width, model_width), jnp.float32),
    )
    dense_out, sum_gate_up, sum_down = lax.fori_loop(0, n_blocks, block_step, start_state)
    back_slots = jnp.where(
        live_rows[:, None], dense_out[jnp.minimum(dense_pos, padded_rows - 1)], 0
    )
    back_slots = back_slots.reshape(n_peers, slot_cap, model_width)
    returned = lax.all_to_all(back_slots, "expert", split_axis=0, concat_axis=0, tiled=True)
    route_parts = returned.reshape(n_slots, model_width)[slot_of_route]
    input_grad = jnp.sum(
        route_parts.reshape(tok_rows, top_k, model_width).astype(jnp.float32), axis=1
    ).astype(jnp.bfloat16)
    share_gate_up = lax.psum_scatter(
        sum_gate_up.astype(jnp.bfloat16), "dp", scatter_dimension=0, tiled=True
    ).astype(jnp.float32)
    share_down = lax.psum_scatter(
        sum_down.astype(jnp.bfloat16), "dp", scatter_dimension=0, tiled=True
    ).astype(jnp.float32)
    grad_gate = (grad_scale * share_gate_up[:, :hidden_width]).astype(jnp.bfloat16)[None]
    grad_up = (grad_scale * share_gate_up[:, hidden_width:]).astype(jnp.bfloat16)[None]
    grad_down = (grad_scale * share_down).astype(jnp.bfloat16)[None]
    return (input_grad, grad_gate, grad_up, grad_down)


def solution(mesh):
    return jax.shard_map(
        local,
        mesh=mesh,
        in_specs=(
            P(("dp", "expert"), None),
            P(("dp", "expert"), None),
            P(("dp", "expert"), None, None),
            P(("dp", "expert"), None),
            P(("dp", "expert"), None),
            P("expert", None, None),
            P("expert", None, None),
            P("expert", None, None),
        ),
        out_specs=(
            P(("dp", "expert"), None),
            P("expert", "dp", None),
            P("expert", "dp", None),
            P("expert", "dp", None),
        ),
        check_vma=False,
    )
```

profile of v0, /device:TPU:0, one launch (start us, length us, event | category | flops | bytes accessed | tf_op | source)
XLA Modules:
  0.0 931.3 jit_solution(2781475931757169068)
XLA Ops:
  33.0 7.6 all-to-all-start.2
  53.9 7.2 fusion.24
  61.1 59.5 %all-to-all-done.2 = bf16[16,96,1408]{2,1,0:T(8,128)(2,1)} async-done(((bf16[16,96,1408]{2,1,0:T(8,128)(2,1)}), bf16[16,96,1408]{2,1,0:T(8,128)(2,1)}, u32[]{:S(2)}, u32[]{:S(2)}) %all-to-all-start.2) | async-done | bytes 4325408 | tf_op jit(solution)/shard_map/all_to_all | solution.py:84
  120.6 20.2 %all-to-all-start = ((bf16[16,96,2048]{2,1,0:T(8,128)(2,1)}), bf16[16,96,2048]{2,1,0:T(8,128)(2,1)}, u32[]{:S(2)}, u32[]{:S(2)}) async-start(bf16[16,96,2048]{2,1,0:T(8,128)(2,1)} %fusion.24), calls=%async_computation | async-start | bytes 12582912 | tf_op jit(solution)/shard_map/all_to_all | solution.py:83
  153.7 101.3 %all-to-all-done = bf16[16,96,2048]{2,1,0:T(8,128)(2,1)} async-done(((bf16[16,96,2048]{2,1,0:T(8,128)(2,1)}), bf16[16,96,2048]{2,1,0:T(8,128)(2,1)}, u32[]{:S(2)}, u32[]{:S(2)}) %all-to-all-start) | async-done | bytes 6291488 | tf_op jit(solution)/shard_map/all_to_all | solution.py:83
  255.0 28.1 %all-to-all-start.1 = ((bf16[16,96,2048]{2,1,0:T(8,128)(2,1)}), bf16[16,96,2048]{2,1,0:T(8,128)(2,1)}, u32[]{:S(2)}, u32[]{:S(2)}) async-start(bf16[16,96,2048]{2,1,0:T(8,128)(2,1)} %broadcast_select_fusion.1), calls=%async_computation.1 | async-start | bytes 12582912 | tf_op jit(solution)/shard_map/all_to_all | solution.py:82
  290.7 11.2 %scatter_custom_fusion.3 = bf16[1536,1408]{1,0:T(8,128)(2,1)} fusion(s32[1536]{0:T(1024)S(1)} %get-tuple-element.68, bf16[1536,1408]{1,0:T(8,128)(2,1)} %bitcast.8, bf16[]{:T(256)} %constant.73.clone.1), kind=kCustom, calls=%fused_computation.60 | custom fusion | bytes 4325888 | tf_op jit(solution)/shard_map/scatter | solution.py:105
  301.9 95.4 %all-to-all-done.1 = bf16[16,96,2048]{2,1,0:T(8,128)(2,1)} async-done(((bf16[16,96,2048]{2,1,0:T(8,128)(2,1)}), bf16[16,96,2048]{2,1,0:T(8,128)(2,1)}, u32[]{:S(2)}, u32[]{:S(2)}) %all-to-all-start.1) | async-done | bytes 6291488 | tf_op jit(solution)/shard_map/all_to_all | solution.py:82
  397.3 14.1 %scatter_custom_fusion.2 = bf16[1536,2048]{1,0:T(8,128)(2,1)} fusion(s32[1536]{0:T(1024)S(1)} %get-tuple-element.68, bf16[1536,2048]{1,0:T(8,128)(2,1)} %bitcast.5, bf16[]{:T(256)} %constant.73.clone.1), kind=kCustom, calls=%fused_computation.53 | custom fusion | bytes 6291968 | tf_op jit(solution)/shard_map/scatter | solution.py:95
  411.5 14.0 %scatter_custom_fusion.1 = bf16[1536,2048]{1,0:T(8,128)(2,1)} fusion(s32[1536]{0:T(1024)S(1)} %get-tuple-element.68, bf16[1536,2048]{1,0:T(8,128)(2,1)} %bitcast.2, bf16[]{:T(256)} %constant.73.clone.1), kind=kCustom, calls=%fused_computation.55 | custom fusion | bytes 6291968 | tf_op jit(solution)/shard_map/scatter | solution.py:100
  434.5 9.1 broadcast_in_dim.88
  443.7 78.8 %while.14 = (s32[]{:T(128)}, bf16[1536,2048]{1,0:T(8,128)(2,1)}, f32[2048,2816]{1,0:T(8,128)}, f32[1408,2048]{1,0:T(8,128)}, s32[]{:T(128)}, /*index=5*/bf16[153...) while((s32[]{:T(128)}, bf16[1536,2048]{1,0:T(8,128)(2,1)}, ...), condition=%wide.region_12.13_spmd, body=%wide.region_11.12_spmd.sunk | while | flops 10354917376 | bytes 175245616 | solution.py:127
  457.4 10.9 %convolution_add_fusion.6 = f32[1408,2048]{1,0:T(8,128)} fusion(f32[1408,2048]{1,0:T(8,128)} %get-tuple-element.189, bf16[1536,2048]{1,0:T(8,128)(2,1)} %get-tuple-element.206, s32[]{:T(128)S(6)} %select_n.129, f32[256,1408]{1,0:T(8,128)S(1)} %fusion.75, bf16[1536,1408]{1,0:T(8,128)(2,1)} %get-tuple-element.210), kind=kOutput, calls=%fused_computation.11.clone.1 | convolution fusion | flops 1481801728 | bytes 26280960 | tf_op jit(solution)/shard_map/while/body/dot_general | solution.py:36
  468.4 14.9 %convolution_add_fusion.5 = f32[2048,2816]{1,0:T(8,128)} fusion(f32[2048,2816]{1,0:T(8,128)} %get-tuple-element.188, bf16[256,1408]{1,0:T(8,128)(2,1)S(1)} %get-tuple-element.170, bf16[256,1408]{1,0:T(8,128)(2,1)S(1)} %get-tuple-element.169, bf16[1536,2048]{1,0:T(8,128)(2,1)} %get-tuple-element.208, s32[]{:T(128)S(6)} %select_n.129), kind=kOutput, calls=%fused_computation.10.clone.1 | convolution fusion | flops 2961440768 | bytes 48627716 | tf_op jit(solution)/shard_map/while/body/dot_general | solution.py:33
  496.7 10.9 %convolution_add_fusion.6 = f32[1408,2048]{1,0:T(8,128)} fusion(f32[1408,2048]{1,0:T(8,128)} %get-tuple-element.189, bf16[1536,2048]{1,0:T(8,128)(2,1)} %get-tuple-element.206, s32[]{:T(128)S(6)} %select_n.129, f32[256,1408]{1,0:T(8,128)S(1)} %fusion.75, bf16[1536,1408]{1,0:T(8,128)(2,1)} %get-tuple-element.210), kind=kOutput, calls=%fused_computation.11.clone.1 | convolution fusion | flops 1481801728 | bytes 26280960 | tf_op jit(solution)/shard_map/while/body/dot_general | solution.py:36
  507.7 14.8 %convolution_add_fusion.5 = f32[2048,2816]{1,0:T(8,128)} fusion(f32[2048,2816]{1,0:T(8,128)} %get-tuple-element.188, bf16[256,1408]{1,0:T(8,128)(2,1)S(1)} %get-tuple-element.170, bf16[256,1408]{1,0:T(8,128)(2,1)S(1)} %get-tuple-element.169, bf16[1536,2048]{1,0:T(8,128)(2,1)} %get-tuple-element.208, s32[]{:T(128)S(6)} %select_n.129), kind=kOutput, calls=%fused_computation.10.clone.1 | convolution fusion | flops 2961440768 | bytes 48627716 | tf_op jit(solution)/shard_map/while/body/dot_general | solution.py:33
  522.5 7.6 convert_element_type.81
  530.4 12.2 %convert_element_type.77 = bf16[2048,2816]{1,0:T(8,128)(2,1)} convert(f32[2048,2816]{1,0:T(8,128)} %get-tuple-element.65) | non-fusion elementwise | flops 5767168 | bytes 34603008 | tf_op jit(solution)/shard_map/convert_element_type | solution.py:138
  543.4 16.3 %gather_fusion.4 = bf16[1536,2048]{1,0:T(8,128)(2,1)} fusion(bf16[1536,2048]{1,0:T(8,128)(2,1)} %get-tuple-element.64, s32[2048]{0:T(1024)S(1)} %pad_clamp_fusion), kind=kCustom, calls=%fused_computation.4 | custom fusion | bytes 12589056 | tf_op jit(solution)/shard_map/gather | solution.py:129
  565.7 185.4 %all-to-all-start.3 = ((bf16[16,96,2048]{2,1,0:T(8,128)(2,1)}), bf16[16,96,2048]{2,1,0:T(8,128)(2,1)}, u32[]{:S(2)}, u32[]{:S(2)}) async-start(bf16[16,96,2048]{2,1,0:T(8,128)(2,1)} %broadcast_select_fusion), calls=%async_computation.3 | async-start | bytes 12582912 | tf_op jit(solution)/shard_map/all_to_all | solution.py:132
  751.1 30.2 %reduce-scatter.5.cloned.1.call-done = bf16[704,2048]{1,0:T(8,128)(2,1)} async-done(((bf16[1408,2048]{1,0:T(8,128)(2,1)}), bf16[704,2048]{1,0:T(8,128)(2,1)}) %reduce-scatter.5.cloned.1.call-update) | async-done | bytes 2883600 | tf_op jit(solution)/shard_map/reduce_scatter | solution.py:140
  785.5 79.8 %all-to-all-done.3 = bf16[16,96,2048]{2,1,0:T(8,128)(2,1)} async-done(((bf16[16,96,2048]{2,1,0:T(8,128)(2,1)}), bf16[16,96,2048]{2,1,0:T(8,128)(2,1)}, u32[]{:S(2)}, u32[]{:S(2)}) %all-to-all-start.3) | async-done | bytes 6291488 | tf_op jit(solution)/shard_map/all_to_all | solution.py:132
  865.3 10.8 %gather_fusion.5 = bf16[768,2048]{1,0:T(8,128)(2,1)} fusion(bf16[1536,2048]{1,0:T(8,128)(2,1)} %bitcast.11, s32[1024]{0:T(1024)S(1)} %pad_clamp_fusion.3), kind=kCustom, calls=%fused_computation.5 | custom fusion | bytes 6294528 | tf_op jit(solution)/shard_map/gather | solution.py:133
  888.1 28.8 %reduce-scatter.3.cloned.1.call-done = bf16[1024,2816]{1,0:T(8,128)(2,1)} async-done(((bf16[2048,2816]{1,0:T(8,128)(2,1)}), bf16[1024,2816]{1,0:T(8,128)(2,1)}) %reduce-scatter.3.cloned.1.call-update) | async-done | bytes 5767184 | tf_op jit(solution)/shard_map/reduce_scatter | solution.py:137
  (98 shorter events, 125.1 us)
Async XLA Ops:
  7.2 39.6 %copy-start = (bf16[128,2048]{1,0:T(8,128)(2,1)S(1)}, bf16[128,2048]{1,0:T(8,128)(2,1)}, u32[]{:S(2)}) copy-start(bf16[128,2048]{1,0:T(8,128)(2,1)} %param.11) | copy-start | bytes 1572868
  11.4 3.5 copy-start.6
  33.0 7.6 copy-start.8
  33.0 87.5 %all-to-all-start.2 = ((bf16[16,96,1408]{2,1,0:T(8,128)(2,1)}), bf16[16,96,1408]{2,1,0:T(8,128)(2,1)}, u32[]{:S(2)}, u32[]{:S(2)}) async-start(bf16[16,96,1408]{2,1,0:T(8,128)(2,1)} %broadcast_select_fusion.2), calls=%async_computation.2 | async-start | bytes 8650752 | tf_op jit(solution)/shard_map/all_to_all | solution.py:84
  61.0 79.7 %copy-start.2 = (bf16[128,2048]{1,0:T(8,128)(2,1)S(1)}, bf16[128,2048]{1,0:T(8,128)(2,1)}, u32[]{:S(2)}) copy-start(bf16[128,2048]{1,0:T(8,128)(2,1)} %param.10) | copy-start | bytes 1572868
  120.6 134.4 %all-to-all-start = ((bf16[16,96,2048]{2,1,0:T(8,128)(2,1)}), bf16[16,96,2048]{2,1,0:T(8,128)(2,1)}, u32[]{:S(2)}, u32[]{:S(2)}) async-start(bf16[16,96,2048]{2,1,0:T(8,128)(2,1)} %fusion.24), calls=%async_computation | async-start | bytes 12582912 | tf_op jit(solution)/shard_map/all_to_all | solution.py:83
  255.0 142.3 %all-to-all-start.1 = ((bf16[16,96,2048]{2,1,0:T(8,128)(2,1)}), bf16[16,96,2048]{2,1,0:T(8,128)(2,1)}, u32[]{:S(2)}, u32[]{:S(2)}) async-start(bf16[16,96,2048]{2,1,0:T(8,128)(2,1)} %broadcast_select_fusion.1), calls=%async_computation.1 | async-start | bytes 12582912 | tf_op jit(solution)/shard_map/all_to_all | solution.py:82
  283.1 498.2 %reduce-scatter.5.cloned.1.call-start = ((), (), s32[]{:S(2)}) async-start(), calls=%async_computation.7 | async-start | bytes 8650752 | tf_op jit(solution)/shard_map/reduce_scatter | solution.py:140
  288.0 1.4 copy-start.3
  443.9 4.9 copy-start.9
  443.9 10.6 %slice-start = ((s8[5767168]{0:T(1024)(128)(4,1)}), s8[4194304]{0:T(1024)(128)(4,1)S(1)}, s32[]{:S(2)}) async-start(s8[5767168]{0:T(1024)(128)(4,1)} %bitcast.73), calls=%async_computation.8 | async-start | bytes 8388608 | tf_op jit(solution)/shard_map/while
  448.8 3.9 copy-start.10
  448.8 5.7 slice-start.1
  483.2 4.9 copy-start.9
  483.2 10.6 %slice-start = ((s8[5767168]{0:T(1024)(128)(4,1)}), s8[4194304]{0:T(1024)(128)(4,1)S(1)}, s32[]{:S(2)}) async-start(s8[5767168]{0:T(1024)(128)(4,1)} %bitcast.73), calls=%async_computation.8 | async-start | bytes 8388608 | tf_op jit(solution)/shard_map/while
  488.1 3.9 copy-start.10
  488.1 5.7 slice-start.1
  530.1 386.8 %reduce-scatter.3.cloned.1.call-start = ((), (), s32[]{:S(2)}) async-start(), calls=%async_computation.6 | async-start | bytes 17301504 | tf_op jit(solution)/shard_map/reduce_scatter | solution.py:137
  542.7 0.7 copy-start.5
  543.4 16.3 %copy-start.4 = (pred[16,96]{1,0:T(8,128)(4,1)S(1)}, pred[16,96]{1,0:T(8,128)(4,1)}, u32[]{:S(2)}) copy-start(pred[16,96]{1,0:T(8,128)(4,1)} %copy-done.3) | copy-start | bytes 4612
  565.7 185.4 %copy-start.7 = (s32[768]{0:T(1024)S(1)}, s32[768]{0:T(1024)}, u32[]{:S(2)}) copy-start(s32[768]{0:T(1024)} %copy-done.6) | copy-start | bytes 9220
  565.7 299.6 %all-to-all-start.3 = ((bf16[16,96,2048]{2,1,0:T(8,128)(2,1)}), bf16[16,96,2048]{2,1,0:T(8,128)(2,1)}, u32[]{:S(2)}, u32[]{:S(2)}) async-start(bf16[16,96,2048]{2,1,0:T(8,128)(2,1)} %broadcast_select_fusion), calls=%async_computation.3 | async-start | bytes 12582912 | tf_op jit(solution)/shard_map/all_to_all | solution.py:132
  916.9 7.1 copy-start.1
Sparse Core Ops, SparseCore 0:
  530.3 250.9 reduce-scatter.4
  783.7 133.1 reduce-scatter.2
where the time goes:
time: 939 us; the launch traced here: 931 us
  waiting for transfers between devices  395 us (42%)
  starting transfers between devices  242 us (26%)
  local copies, waits for them, and re-layouts  132 us (14%)
  matrix products  78.4 us (8%)
  other arithmetic  68.5 us (7%)
  between operations  15.4 us (2%)
    all_to_all x1, starting transfers between devices, local(): lax.all_to_all(back_slots, 'expert', split_axis=0, concat_axis=0, tiled=T...  185 us
    all_to_all x1, waiting for transfers between devices, local(): lax.all_to_all(send_grad, 'expert', split_axis=0, concat_axis=0, tiled=True)  101 us
    all_to_all x1, waiting for transfers between devices, local(): lax.all_to_all(send_rows, 'expert', split_axis=0, concat_axis=0, tiled=True)  95.4 us
    all_to_all x1, waiting for transfers between devices, local(): lax.all_to_all(back_slots, 'expert', split_axis=0, concat_axis=0, tiled=T...  79.8 us
    all_to_all x1, waiting for transfers between devices, local(): lax.all_to_all(send_gate, 'expert', split_axis=0, concat_axis=0, tiled=True)  59.5 us
    reduce_scatter x1, waiting for transfers between devices, local(): lax.psum_scatter(sum_down.astype(jnp.bfloat16), 'dp', scatter_dimension=0...  30.2 us
    dot_general x2, matrix products, weight_terms(): lax.dot_general(rows_in, both_grads, contract_rows, preferred_element_typ...  29.7 us
    reduce_scatter x1, waiting for transfers between devices, local(): lax.psum_scatter(sum_gate_up.astype(jnp.bfloat16), 'dp', scatter_dimensio...  28.8 us
  transfers between devices with their start and end apart: 6, of which 6 were waited for; matrix products, arithmetic and copies ran while one was open for 12% of the time, Pallas kernels for 0%

commit v1 on v0

v1 whole, which is shorter than its diff:
```python
import jax
import jax.numpy as jnp
from jax import lax
from jax.sharding import PartitionSpec as P

grad_scale = 0.0625
f32 = jnp.float32
bf16 = jnp.bfloat16


def dot(a, b, dims):
    return lax.dot_general(a, b, (dims, ((), ())), preferred_element_type=f32)


def chunk_widths(width):
    lanes = width // 128
    n = 4 if lanes >= 8 else 1
    sizes = [lanes // n + (1 if i >= n - lanes % n else 0) for i in range(n)]
    return [s * 128 for s in sizes]


def local(tokens, out_grad, gate_saved, probs, expert_ids, w_gate, w_up, w_down):
    n_peers = lax.axis_size("expert")
    n_dp = lax.axis_size("dp")
    me = lax.axis_index("expert")
    group = lax.axis_index("dp")
    tok_rows, model_width = tokens.shape
    top_k = expert_ids.shape[1]
    hidden_width = w_up.shape[2]
    cap = min(tok_rows, 2 * tok_rows * top_k // n_peers)
    n_routes = tok_rows * top_k
    n_slots = n_peers * cap
    gate_mat, up_mat, down_mat = w_gate[0], w_up[0], w_down[0]

    meta = jnp.concatenate([expert_ids.astype(f32), probs], axis=1)
    meta_all = lax.all_gather(meta, "expert", axis=0, tiled=False)
    tok_all = lax.all_gather(tokens, "expert", axis=0, tiled=False)
    grad_all = lax.all_gather(out_grad, "expert", axis=0, tiled=False)

    experts = jnp.arange(n_peers, dtype=jnp.int32)
    hit = expert_ids[:, :, None] == experts[None, None, :]
    named = jnp.any(hit, axis=1)
    rank = jnp.cumsum(named.astype(jnp.int32), axis=0) - 1
    slots = jnp.arange(cap, dtype=jnp.int32)
    pick = (
        hit[:, :, :, None] & (rank[:, None, :, None] == slots[None, None, None, :])
    ).astype(bf16)
    send_gate = lax.dot_general(
        pick.reshape(n_routes, n_slots),
        gate_saved.reshape(n_routes, hidden_width),
        (((0,), (0,)), ((), ())),
        preferred_element_type=f32,
    ).astype(bf16).reshape(n_peers, cap, hidden_width)

    widths = chunk_widths(hidden_width)
    starts = [sum(widths[:i]) for i in range(len(widths))]
    recv_gate = [
        lax.all_to_all(
            send_gate[:, :, s : s + w], "expert", split_axis=0, concat_axis=0, tiled=True
        ).reshape(n_slots, w)
        for s, w in zip(starts, widths)
    ]

    ids_all = meta_all[:, :, :top_k].astype(jnp.int32)
    mine = ids_all == me
    prob_all = jnp.sum(jnp.where(mine, meta_all[:, :, top_k:], 0.0), axis=2)
    mine = jnp.any(mine, axis=2)
    rank_all = jnp.cumsum(mine.astype(jnp.int32), axis=1) - 1
    place = (
        mine[:, None, :] & (rank_all[:, None, :] == slots[None, :, None])
    ).astype(bf16)
    by_block = (((2,), (1,)), ((0,), (0,)))
    rows_in = (
        lax.dot_general(place, tok_all, by_block, preferred_element_type=f32)
        .astype(bf16)
        .reshape(n_slots, model_width)
    )
    scaled = (prob_all[:, :, None] * grad_all.astype(f32)).astype(bf16)
    routed = (
        lax.dot_general(place, scaled, by_block, preferred_element_type=f32)
        .astype(bf16)
        .reshape(n_slots, model_width)
    )

    up_act = dot(rows_in, up_mat, ((1,), (0,)))
    hidden_grad = dot(routed, down_mat, ((1,), (1,)))

    piece = model_width // n_dp
    shifts = [[(i, (i + d) % n_dp) for i in range(n_dp)] for d in range(n_dp)]

    def rows_of(d):
        q = lax.rem(group + d, n_dp)
        return lax.dynamic_slice_in_dim(rows_in, q * piece, piece, 1)

    gate_out, up_out, hidden_parts, gate_parts, up_parts = [], [], [], [], []
    for s, w, gate_rows in zip(starts, widths, recv_gate):
        gate_val = gate_rows.astype(f32)
        gate_sig = jax.nn.sigmoid(gate_val)
        gate_act = gate_val * gate_sig
        up_c = up_act[:, s : s + w]
        grad_c = hidden_grad[:, s : s + w]
        hidden_parts.append((gate_act * up_c).astype(bf16))
        up_grad = (grad_c * gate_act).astype(bf16)
        gate_grad = (grad_c * up_c * gate_sig * (1.0 + gate_val * (1.0 - gate_sig))).astype(bf16)
        gate_parts.append(gate_grad)
        up_parts.append(up_grad)
        both = jnp.concatenate([gate_grad, up_grad], axis=1)
        arrived = []
        for d in range(1, n_dp):
            part = dot(rows_of(d), both, ((0,), (0,))).astype(bf16)
            arrived.append(lax.ppermute(part, "dp", shifts[d]))
        total = dot(rows_of(0), both, ((0,), (0,))).astype(bf16).astype(f32)
        for part in arrived:
            total = total + part.astype(f32)
        total = (grad_scale * total).astype(bf16)
        gate_out.append(total[:, :w])
        up_out.append(total[:, w:])

    hidden_act = jnp.concatenate(hidden_parts, axis=1)
    sum_down = dot(hidden_act, routed, ((0,), (0,))).astype(bf16)
    low = hidden_width // n_dp
    arrived = []
    for d in range(1, n_dp):
        q = lax.rem(group + d, n_dp)
        part = lax.dynamic_slice_in_dim(sum_down, q * low, low, 0)
        arrived.append(lax.ppermute(part, "dp", shifts[d]))
    down = lax.dynamic_slice_in_dim(sum_down, group * low, low, 0).astype(f32)
    for part in arrived:
        down = down + part.astype(f32)
    grad_down = (grad_scale * down).astype(bf16)[None]

    gate_grad = jnp.concatenate(gate_parts, axis=1)
    up_grad = jnp.concatenate(up_parts, axis=1)
    input_part = (
        (dot(gate_grad, gate_mat, ((1,), (1,))) + dot(up_grad, up_mat, ((1,), (1,))))
        .astype(bf16)
        .reshape(n_peers, cap, model_width)
    )
    spread = lax.dot_general(
        place, input_part, (((1,), (1,)), ((0,), (0,))), preferred_element_type=f32
    ).astype(bf16)
    input_grad = lax.psum_scatter(
        spread.reshape(n_peers * tok_rows, model_width), "expert", scatter_dimension=0, tiled=True
    )
    grad_gate = jnp.concatenate(gate_out, axis=1)[None]
    grad_up = jnp.concatenate(up_out, axis=1)[None]
    return (input_grad, grad_gate, grad_up, grad_down)


def solution(mesh):
    return jax.shard_map(
        local,
        mesh=mesh,
        in_specs=(
            P(("dp", "expert"), None),
            P(("dp", "expert"), None),
            P(("dp", "expert"), None, None),
            P(("dp", "expert"), None),
            P(("dp", "expert"), None),
            P("expert", None, None),
            P("expert", None, None),
            P("expert", None, None),
        ),
        out_specs=(
            P(("dp", "expert"), None),
            P("expert", "dp", None),
            P("expert", "dp", None),
            P("expert", "dp", None),
        ),
        check_vma=False,
    )
```

time: 939 us -> 546 us (0.58)
  the two profiles are of different devices: /device:TPU:0 before, /device:TPU:12 now
where the time goes in v1:
time: 546 us; the launch traced here: 538 us
  waiting for transfers between devices  202 us (37%)
  matrix products  136 us (25%)
  blocking collectives  99.8 us (18%)
  local copies, waits for them, and re-layouts  35.4 us (6%)
  other arithmetic  26.9 us (5%)
  starting transfers between devices  23.7 us (4%)
  between operations  14.6 us (3%)
    ppermute x5, waiting for transfers between devices, local(): arrived.append(lax.ppermute(part, 'dp', shifts[d]))  131 us
    dot_general x13, matrix products, dot(): return lax.dot_general(a, b, (dims, ((), ())), preferred_element_type=f32)  106 us
    all_to_all x3, waiting for transfers between devices, local(): lax.all_to_all(send_gate[:, :, s:s + w], 'expert', split_axis=0, concat_a...  69.2 us
    all_gather x1, blocking collectives, local(): meta_all = lax.all_gather(meta, 'expert', axis=0, tiled=False)  54.3 us
    all_to_all x1, blocking collectives, local(): lax.all_to_all(send_gate[:, :, s:s + w], 'expert', split_axis=0, concat_a...  45.5 us
    all_to_all x3, starting transfers between devices, local(): lax.all_to_all(send_gate[:, :, s:s + w], 'expert', split_axis=0, concat_a...  17.9 us
    unnamed x67, local copies, waits for them, and re-layouts  14.6 us
  transfers between devices with their start and end apart: 11, of which 6 were waited for; matrix products, arithmetic and copies ran while one was open for 19% of the time, Pallas kernels for 0%

profile of v1, /device:TPU:12, one launch (start us, length us, event | category | flops | bytes accessed | tf_op | source)
XLA Modules:
  0.0 538.0 jit_solution(11060954787428533356)
XLA Ops:
  21.5 5.8 %convolution_convert_fusion.1 = bf16[1536,1408]{1,0:T(8,128)(2,1)S(1)} fusion(pred[768,1536]{1,0:T(32,128)(4,1)} %and.40, bf16[768,1408]{1,0:T(8,128)(2,1)} %reshape.84), kind=kOutput, calls=%fused_computation.6 | convolution fusion | flops 3324051456 | bytes 7667712 | tf_op jit(solution)/shard_map/dot_general | solution.py:48
  30.3 6.2 %all-to-all-start = ((bf16[16,96,256]{2,1,0:T(8,128)(2,1)}), bf16[16,96,256]{2,1,0:T(8,128)(2,1)S(1)}, u32[]{:S(2)}, u32[]{:S(2)}) async-start(bf16[16,96,256]{2,1,0:T(8,128)(2,1)} %slice.92), calls=%async_computation | async-start | bytes 1572864 | tf_op jit(solution)/shard_map/all_to_all | solution.py:58
  40.4 29.5 %all-to-all-done = bf16[16,96,256]{2,1,0:T(8,128)(2,1)S(1)} async-done(((bf16[16,96,256]{2,1,0:T(8,128)(2,1)}), bf16[16,96,256]{2,1,0:T(8,128)(2,1)S(1)}, u32[]{:S(2)}, u32[]{:S(2)}) %all-to-all-start) | async-done | bytes 786464 | tf_op jit(solution)/shard_map/all_to_all | solution.py:58
  69.9 45.5 %all_to_all.20 = bf16[16,96,384]{2,1,0:T(8,128)(2,1)S(1)} all-to-all(bf16[16,96,384]{2,1,0:T(8,128)(2,1)S(1)} %get-tuple-element.27), channel_id=1, replica_groups=mesh['dp'=2,'expert'=16] {'expert'}, dimensions={0} | all-to-all | bytes 2359296 | tf_op jit(solution)/shard_map/all_to_all | solution.py:58
  115.4 5.4 all-to-all-start.2
  120.8 54.3 %all-gather = f32[2048,12]{0,1:T(8,128)S(1)} all-gather(f32[128,12]{0,1:T(8,128)S(1)} %pad_maximum_fusion.18), channel_id=2, replica_groups=mesh['dp'=2,'expert'=16] {'expert'}, dimensions={0}, use_global_device_ids=true | all-gather | bytes 104448 | tf_op jit(solution)/shard_map/all_gather | solution.py:36
  175.1 6.3 %all-to-all-start.1 = ((bf16[16,96,384]{2,1,0:T(8,128)(2,1)}), bf16[16,96,384]{2,1,0:T(8,128)(2,1)}, u32[]{:S(2)}, u32[]{:S(2)}) async-start(bf16[16,96,384]{2,1,0:T(8,128)(2,1)} %get-tuple-element.26), calls=%async_computation.1 | async-start | bytes 2359296 | tf_op jit(solution)/shard_map/all_to_all | solution.py:58
  190.0 39.7 %all-to-all-done.1 = bf16[16,96,384]{2,1,0:T(8,128)(2,1)} async-done(((bf16[16,96,384]{2,1,0:T(8,128)(2,1)}), bf16[16,96,384]{2,1,0:T(8,128)(2,1)}, u32[]{:S(2)}, u32[]{:S(2)}) %all-to-all-start.1) | async-done | bytes 1179680 | tf_op jit(solution)/shard_map/all_to_all | solution.py:58
  233.1 7.8 %convolution_convert_fusion.3 = bf16[16,96,2048]{2,1,0:T(8,128)(2,1)} fusion(bf16[16,128,2048]{2,1,0:T(8,128)(2,1)} %bitcast.53, s32[16,128]{1,0:T(8,128)S(1)} %broadcast_add_fusion.1, pred[16,128]{1,0:T(8,128)(4,1)S(1)} %reduce_or.18), kind=kOutput, calls=%fused_computation.16 | convolution fusion | flops 808845312 | bytes 14690304 | tf_op jit(solution)/shard_map/dot_general | solution.py:74
  240.9 8.2 %fusion.11 = bf16[16,96,2048]{2,1,0:T(8,128)(2,1)} fusion(bf16[16,128,2048]{2,1,0:T(8,128)(2,1)} %bitcast.67, f32[16,128]{1,0:T(8,128)S(1)} %copy-done.22, s32[16,128]{1,0:T(8,128)S(1)} %broadcast_add_fusion.1, pred[16,128]{1,0:T(8,128)(4,1)S(1)} %reduce_or.18), kind=kOutput, calls=%fused_computation.17 | convolution fusion | flops 821428224 | bytes 14698496 | tf_op jit(solution)/shard_map/dot_general | solution.py:80
  249.1 13.4 %fusion.9 = f32[1536,1408]{0,1:T(8,128)S(1)} fusion(bf16[1536,2048]{1,0:T(8,128)(2,1)} %bitcast.69, bf16[1,1408,2048]{2,1,0:T(8,128)(2,1)} %param.15), kind=kOutput, calls=%fused_computation.12 | convolution fusion | flops 8858370048 | bytes 20709376 | tf_op jit(solution)/shard_map/dot_general | solution.py:12
  262.5 15.1 %fusion.7 = f32[1536,1408]{0,1:T(8,128)} fusion(bf16[1536,2048]{1,0:T(8,128)(2,1)S(1)} %bitcast.57, bf16[1,2048,1408]{2,1,0:T(8,128)(2,1)} %param.14), kind=kOutput, calls=%fused_computation.10 | convolution fusion | flops 8858370048 | bytes 20709376 | tf_op jit(solution)/shard_map/dot_general | solution.py:12
  281.5 8.2 %multiply_convert_fusion.12 = (bf16[1536,384]{0,1:T(8,128)(2,1)S(1)}, bf16[1536,384]{0,1:T(8,128)(2,1)S(1)}, bf16[1536,384]{0,1:T(8,128)(2,1)S(1)}, bf16[1536,38...) fusion(f32[1536,384]{0,1:T(8,128)S(1)} %copy-done.2, ...), kind=kLoop, calls=%fused_computation.61 | loop fusion | flops 26542080 | bytes 31850496 | tf_op jit(solution)/shard_map/convert_element_type | solution.py:104
  289.7 16.4 %fusion.4 = f32[1536,2048]{1,0:T(8,128)} fusion(bf16[1,2048,1408]{2,1,0:T(8,128)(2,1)} %param.13, bf16[1536,384]{0,1:T(8,128)(2,1)S(1)} %get-tuple-element.15, bf16[1536,384]{0,1:T(8,128)(2,1)S(1)} %get-tuple-element.16, bf16[1536,384]{0,1:T(8,128)(2,1)S(1)} %get-tuple-element.14, bf16[1536,256]{0,1:T(8,128)(2,1)S(1)} %get-tuple-element.24), kind=kOutput, calls=%fused_computation.7 | convolution fusion | flops 8875671552 | bytes 22675456 | tf_op jit(solution)/shard_map/dot_general | solution.py:12
  306.2 17.0 %add_convert_fusion = bf16[1536,2048]{1,0:T(8,128)(2,1)} fusion(f32[1536,2048]{1,0:T(8,128)} %fusion.4, bf16[1,2048,1408]{2,1,0:T(8,128)(2,1)} %param.14, bf16[1536,384]{0,1:T(8,128)(2,1)} %get-tuple-element.20, bf16[1536,384]{0,1:T(8,128)(2,1)} %get-tuple-element.19, bf16[1536,384]{0,1:T(8,128)(2,1)S(1)} %get-tuple-element.22, ...), kind=kOutput, calls=%fused_computation.2 | convolution fusion | flops 8881963008 | bytes 28966912 | tf_op jit(solution)/shard_map/dot_general | solution.py:12
  323.2 8.5 %convolution_convert_fusion.2 = bf16[16,128,2048]{2,1,0:T(8,128)(2,1)} fusion(bf16[16,96,2048]{2,1,0:T(8,128)(2,1)} %bitcast.68, s32[16,128]{1,0:T(8,128)S(1)} %broadcast_add_fusion.1, pred[16,128]{1,0:T(8,128)(4,1)S(1)} %reduce_or.18), kind=kOutput, calls=%fused_computation.15 | convolution fusion | flops 809893888 | bytes 14690304 | tf_op jit(solution)/shard_map/dot_general | solution.py:139
  331.7 5.3 fusion.77
  352.1 12.6 %convolution_convert_fusion = bf16[1408,2048]{1,0:T(8,128)(2,1)S(1)} fusion(bf16[1536,2048]{1,0:T(8,128)(2,1)S(1)} %bitcast.72, bf16[1536,384]{0,1:T(8,128)(2,1)} %get-tuple-element.18, bf16[1536,384]{0,1:T(8,128)(2,1)} %get-tuple-element.17, bf16[1536,384]{0,1:T(8,128)(2,1)} %get-tuple-element.21, bf16[1536,256]{0,1:T(8,128)(2,1)S(1)} %copy-done.21), kind=kOutput, calls=%fused_computation.5 | convolution fusion | flops 8878555136 | bytes 16384000 | tf_op jit(solution)/shard_map/dot_general | solution.py:12
  372.7 24.3 %collective-permute-done.2 = bf16[1024,768]{0,1:T(8,128)(2,1)} collective-permute-done((bf16[1024,768]{0,1:T(8,128)(2,1)}, bf16[1024,768]{0,1:T(8,128)(2,1)}, u32[]{:S(2)}, u32[]{:S(2)}) %collective-permute-start.2) | collective-permute-done | bytes 1572896 | tf_op jit(solution)/shard_map/ppermute | solution.py:111
  401.1 29.6 %collective-permute-done.3 = bf16[1024,768]{0,1:T(8,128)(2,1)} collective-permute-done((bf16[1024,768]{0,1:T(8,128)(2,1)}, bf16[1024,768]{0,1:T(8,128)(2,1)}, u32[]{:S(2)}, u32[]{:S(2)}) %collective-permute-start.3) | collective-permute-done | bytes 1572896 | tf_op jit(solution)/shard_map/ppermute | solution.py:111
  434.8 29.6 %collective-permute-done.1 = bf16[1024,768]{0,1:T(8,128)(2,1)} collective-permute-done((bf16[1024,768]{0,1:T(8,128)(2,1)}, bf16[1024,768]{0,1:T(8,128)(2,1)}, u32[]{:S(2)}, u32[]{:S(2)}) %collective-permute-start.1) | collective-permute-done | bytes 1572896 | tf_op jit(solution)/shard_map/ppermute | solution.py:111
  470.4 4.5 copy.41
  477.8 47.6 %collective-permute-done.4 = bf16[704,2048]{1,0:T(8,128)(2,1)} collective-permute-done((bf16[704,2048]{1,0:T(8,128)(2,1)}, bf16[704,2048]{1,0:T(8,128)(2,1)}, u32[]{:S(2)}, u32[]{:S(2)}) %collective-permute-start.4) | collective-permute-done | bytes 2883616 | tf_op jit(solution)/shard_map/ppermute | solution.py:126
  525.4 5.7 %fusion.35 = bf16[1,704,2048]{2,1,0:T(8,128)(2,1)} fusion(bf16[704,2048]{1,0:T(8,128)(2,1)} %collective-permute-done.4, bf16[1408,2048]{1,0:T(8,128)(2,1)} %copy-done.4, s32[]{:T(128)S(6)} %select_n.25), kind=kLoop, calls=%fused_computation.43 | loop fusion | flops 7208960 | bytes 8650756 | tf_op jit(solution)/shard_map/broadcast_in_dim | solution.py:130
  (125 shorter events, 77.1 us)
Async XLA Ops:
  7.2 225.9 %all-gather.8.cloned.1.call-start = ((), (), s32[]{:S(2)}) async-start(), calls=%async_computation.7 | async-start | bytes 8912896 | tf_op jit(solution)/shard_map/all_gather | solution.py:37
  7.9 233.0 %all-gather.6.cloned.1.call-start = ((), (), s32[]{:S(2)}) async-start(), calls=%async_computation.6 | async-start | bytes 8912896 | tf_op jit(solution)/shard_map/all_gather | solution.py:38
  30.3 39.6 %all-to-all-start = ((bf16[16,96,256]{2,1,0:T(8,128)(2,1)}), bf16[16,96,256]{2,1,0:T(8,128)(2,1)S(1)}, u32[]{:S(2)}, u32[]{:S(2)}) async-start(bf16[16,96,256]{2,1,0:T(8,128)(2,1)} %slice.92), calls=%async_computation | async-start | bytes 1572864 | tf_op jit(solution)/shard_map/all_to_all | solution.py:58
  40.4 80.3 %copy-start.23 = (s32[128,6]{0,1:T(8,128)S(1)}, s32[128,6]{0,1:T(8,128)}, u32[]{:S(2)}) copy-start(s32[128,6]{0,1:T(8,128)} %param.12) | copy-start | bytes 9220
  40.4 80.3 %copy-start.24 = (f32[128,6]{0,1:T(8,128)S(1)}, f32[128,6]{0,1:T(8,128)}, u32[]{:S(2)}) copy-start(f32[128,6]{0,1:T(8,128)} %param.11) | copy-start | bytes 9220
  115.4 59.7 %all-to-all-start.2 = ((bf16[16,96,384]{2,1,0:T(8,128)(2,1)}), bf16[16,96,384]{2,1,0:T(8,128)(2,1)S(1)}, u32[]{:S(2)}, u32[]{:S(2)}) async-start(bf16[16,96,384]{2,1,0:T(8,128)(2,1)} %get-tuple-element.28), calls=%async_computation.2 | async-start | bytes 2359296 | tf_op jit(solution)/shard_map/all_to_all | solution.py:58
  175.1 54.6 %all-to-all-start.1 = ((bf16[16,96,384]{2,1,0:T(8,128)(2,1)}), bf16[16,96,384]{2,1,0:T(8,128)(2,1)}, u32[]{:S(2)}, u32[]{:S(2)}) async-start(bf16[16,96,384]{2,1,0:T(8,128)(2,1)} %get-tuple-element.26), calls=%async_computation.1 | async-start | bytes 2359296 | tf_op jit(solution)/shard_map/all_to_all | solution.py:58
  181.4 349.7 %reduce-scatter.2.cloned.1.call-start = ((), (), s32[]{:S(2)}) async-start(), calls=%async_computation.5 | async-start | bytes 8912896 | tf_op jit(solution)/shard_map/reduce_scatter | solution.py:142
  240.9 21.6 %slice-start = ((s8[6291456]{0:T(1024)(128)(4,1)}), s8[4194304]{0:T(1024)(128)(4,1)S(1)}, s32[]{:S(2)}) async-start(s8[6291456]{0:T(1024)(128)(4,1)} %bitcast.55), calls=%async_computation.8 | async-start | bytes 8388608
  249.1 13.4 %slice-start.1 = ((s8[6291456]{0:T(1024)(128)(4,1)}), s8[2097152]{0:T(1024)(128)(4,1)S(1)}, s32[]{:S(2)}) async-start(s8[6291456]{0:T(1024)(128)(4,1)} %bitcast.55), calls=%async_computation.9 | async-start | bytes 4194304
  262.5 15.2 %copy-start.3 = (f32[1536,256]{0,1:T(8,128)S(1)}, f32[1536,256]{0,1:T(8,128)}, u32[]{:S(2)}) copy-start(f32[1536,256]{0,1:T(8,128)} %copy.25) | copy-start | bytes 4718596
  281.5 8.2 %copy-start.17 = (bf16[1536,256]{0,1:T(8,128)(2,1)}, bf16[1536,256]{0,1:T(8,128)(2,1)S(1)}, u32[]{:S(2)}) copy-start(bf16[1536,256]{0,1:T(8,128)(2,1)S(1)} %get-tuple-element.24) | copy-start | bytes 2359300
  289.7 16.4 %copy-start.9 = (bf16[1536,384]{0,1:T(8,128)(2,1)}, bf16[1536,384]{0,1:T(8,128)(2,1)S(1)}, u32[]{:S(2)}) copy-start(bf16[1536,384]{0,1:T(8,128)(2,1)S(1)} %get-tuple-element.15) | copy-start | bytes 3538948
  289.7 16.4 %copy-start.12 = (bf16[1536,384]{0,1:T(8,128)(2,1)}, bf16[1536,384]{0,1:T(8,128)(2,1)S(1)}, u32[]{:S(2)}) copy-start(bf16[1536,384]{0,1:T(8,128)(2,1)S(1)} %get-tuple-element.16) | copy-start | bytes 3538948
  289.7 16.4 %copy-start.7 = (bf16[1536,384]{0,1:T(8,128)(2,1)}, bf16[1536,384]{0,1:T(8,128)(2,1)S(1)}, u32[]{:S(2)}) copy-start(bf16[1536,384]{0,1:T(8,128)(2,1)S(1)} %get-tuple-element.22) | copy-start | bytes 3538948
  289.7 16.4 %copy-start.19 = (bf16[1536,256]{0,1:T(8,128)(2,1)S(1)}, bf16[1536,256]{0,1:T(8,128)(2,1)}, u32[]{:S(2)}) copy-start(bf16[1536,256]{0,1:T(8,128)(2,1)} %get-tuple-element.25) | copy-start | bytes 2359300
  337.0 32.6 %collective-permute-start = (bf16[1024,512]{0,1:T(8,128)(2,1)}, bf16[1024,512]{0,1:T(8,128)(2,1)}, u32[]{:S(2)}, u32[]{:S(2)}) collective-permute-start(bf16[1024,512]{0,1:T(8,128)(2,1)} %fusion.77), channel_id=1, source_target_pairs={{0,16},{16,0},{1,17},{17,1},{2,18},{18,2},{3,19},{19,3},{4,20},{20... | collective-permute-start | bytes 3145736 | tf_op jit(solution)/shard_map/ppermute | solution.py:111
  342.2 54.8 %collective-permute-start.2 = (bf16[1024,768]{0,1:T(8,128)(2,1)}, bf16[1024,768]{0,1:T(8,128)(2,1)}, u32[]{:S(2)}, u32[]{:S(2)}) collective-permute-start(bf16[1024,768]{0,1:T(8,128)(2,1)} %fusion.67), channel_id=1, source_target_pairs={{0,16},{16,0},{1,17},{17,1},{2,18},{18,2},{3,19},{19,3},{4,20},{20... | collective-permute-start | bytes 4718600 | tf_op jit(solution)/shard_map/ppermute | solution.py:111
  342.7 9.4 %slice-start.4 = ((s8[6291456]{0:T(1024)(128)(4,1)}), s8[4194304]{0:T(1024)(128)(4,1)S(1)}, s32[]{:S(2)}) async-start(s8[6291456]{0:T(1024)(128)(4,1)} %bitcast.70), calls=%async_computation.12 | async-start | bytes 8388608
  346.4 84.3 %collective-permute-start.3 = (bf16[1024,768]{0,1:T(8,128)(2,1)}, bf16[1024,768]{0,1:T(8,128)(2,1)}, u32[]{:S(2)}, u32[]{:S(2)}) collective-permute-start(bf16[1024,768]{0,1:T(8,128)(2,1)} %fusion.64), channel_id=1, source_target_pairs={{0,16},{16,0},{1,17},{17,1},{2,18},{18,2},{3,19},{19,3},{4,20},{20... | collective-permute-start | bytes 4718600 | tf_op jit(solution)/shard_map/ppermute | solution.py:111
  351.6 112.9 %collective-permute-start.1 = (bf16[1024,768]{0,1:T(8,128)(2,1)}, bf16[1024,768]{0,1:T(8,128)(2,1)}, u32[]{:S(2)}, u32[]{:S(2)}) collective-permute-start(bf16[1024,768]{0,1:T(8,128)(2,1)} %fusion.70), channel_id=1, source_target_pairs={{0,16},{16,0},{1,17},{17,1},{2,18},{18,2},{3,19},{19,3},{4,20},{20... | collective-permute-start | bytes 4718600 | tf_op jit(solution)/shard_map/ppermute | solution.py:111
  368.1 28.9 %copy-start.14 = (bf16[1536,384]{0,1:T(8,128)(2,1)S(1)}, bf16[1536,384]{0,1:T(8,128)(2,1)}, u32[]{:S(2)}) copy-start(bf16[1536,384]{0,1:T(8,128)(2,1)} %copy-done.12) | copy-start | bytes 3538948
  368.1 28.9 %copy-start.16 = (bf16[1536,384]{0,1:T(8,128)(2,1)S(1)}, bf16[1536,384]{0,1:T(8,128)(2,1)}, u32[]{:S(2)}) copy-start(bf16[1536,384]{0,1:T(8,128)(2,1)} %get-tuple-element.19) | copy-start | bytes 3538948
  368.1 157.3 %collective-permute-start.4 = (bf16[704,2048]{1,0:T(8,128)(2,1)}, bf16[704,2048]{1,0:T(8,128)(2,1)}, u32[]{:S(2)}, u32[]{:S(2)}) collective-permute-start(bf16[704,2048]{1,0:T(8,128)(2,1)} %constant_dynamic-slice_fusion), channel_id=1, source_target_pairs={{0,16},{16,0},{1,17},{17,1},{2,18},{18,2},{3,19},{19,3},{4,20},{20... | collective-permute-start | bytes 8650760 | tf_op jit(solution)/shard_map/ppermute | solution.py:126
  (18 other events, 97.8 us)
Sparse Core Ops, SparseCore 0:
  10.2 97.6 all-gather.7
  110.0 115.7 all-gather.5
  331.8 104.4 reduce-scatter.1
